TPU v7x, 32 devices: a whole 2x2x4 slice. The times are simulated.
32 devices in a mesh: groups: 2 (over y), expert: 4 (over z), tensor: 2 (over x), dp: 2 (over core).
Axes of the slice: x: 2, y: 2, z: 4, core: 2. Of those that a mesh axis runs over, the one named last changes fastest.
Arguments:
- tokens: bfloat16 [1536, 7168], P(('groups', 'expert', 'dp'), 'tensor'), parts along dimension 0, may hold values from -6 to 6
- route_weight: bfloat16 [1536], P(('groups', 'expert', 'dp')), parts along dimension 0, may hold values from 0.25 to 1
- block_start: int32 [16, 2], P(('groups', 'expert', 'dp')), parts along dimension 0, may hold values from 0 to 96, as said below
- block_count: int32 [16, 2], P(('groups', 'expert', 'dp')), parts along dimension 0, may hold values from 0 to 64
- spill_rows: int32 [16, 2, 32], P(('groups', 'expert', 'dp')), parts along dimension 0, may hold values from 0 to 95
- spill_count: int32 [16, 2], P(('groups', 'expert', 'dp')), parts along dimension 0, may hold values from 0 to 32
- in_weights: bfloat16 [2, 7168, 2, 2048], P(None, 'expert', None, ('tensor', 'dp')), may hold values from -0.0625 to 0.0625
- out_weights: bfloat16 [2, 2048, 7168], P(None, ('tensor', 'dp'), 'expert'), may hold values from -0.125 to 0.125
Outputs:
- layer_out: bfloat16 [1536, 7168], P(('groups', 'expert', 'dp'), 'tensor'), parts along dimension 0
There are 2 independent parts, one for each index of `groups`. A program takes and returns all parts, laid end to end along the dimension named above; an argument that names none is the same for every part. Nothing has to cross between parts.
Inputs may be any that keep to these rules, and one draw needn't show every extreme that they name: In every shard the rows are ordered by first-choice expert: expert 0's block starts at row 0, expert 1's at block_start; block_count is that block's size capped at 64. The rows of a block past 64 are the first spill_count entries of the other expert's spill_rows, in some order; the other entries are 0. Each token is served by exactly one live slot. Some shard of every draw puts all 96 rows into expert 0's block.
All inputs are finite; a program needn't handle non-finite values.
Results may differ from a plain program's by a relative error of at most 0.009.
Values may be sent and summed in bfloat16 or wider, within the bound.
A program may use at most 192 MiB of HBM per device.

v0:
```python
import jax
import jax.numpy as jnp
from jax import lax
from jax.sharding import PartitionSpec as P


def slot_plan(starts, counts, spills, spill_counts, rows_each):
    overflow = spills.shape[-1]
    capacity = rows_each - overflow
    first_pos = jnp.arange(capacity, dtype=jnp.int32)
    spill_pos = jnp.arange(overflow, dtype=jnp.int32)
    block_rows = starts[..., None].astype(jnp.int32) + first_pos
    slot_rows = jnp.clip(
        jnp.concatenate([block_rows, spills.astype(jnp.int32)], axis=-1), 0, rows_each - 1
    )
    slot_live = jnp.concatenate(
        [first_pos < counts[..., None], spill_pos < spill_counts[..., None]], axis=-1
    )
    return (slot_rows, slot_live)


def local(
    tokens, route_weight, block_start, block_count, spill_rows, spill_count, in_weights, out_weights
):
    rows_each, local_cols = tokens.shape
    tensor_count = lax.axis_size("tensor")
    share_count = lax.axis_size("dp")
    expert_count = in_weights.shape[0]
    hidden_width = in_weights.shape[3]
    gathered = (
        lax.all_gather(tokens[None], ("tensor", "dp"), axis=0, tiled=True),
        lax.all_gather(route_weight[None], ("tensor", "dp"), axis=0, tiled=True),
        lax.all_gather(block_start[None], ("tensor", "dp"), axis=0, tiled=True),
        lax.all_gather(block_count[None], ("tensor", "dp"), axis=0, tiled=True),
        lax.all_gather(spill_rows[None], ("tensor", "dp"), axis=0, tiled=True),
        lax.all_gather(spill_count[None], ("tensor", "dp"), axis=0, tiled=True),
    )
    features = gathered[0].reshape(tensor_count, share_count, rows_each, local_cols)
    features = features.transpose(1, 2, 0, 3).reshape(
        share_count * rows_each, tensor_count * local_cols
    )
    weighting = gathered[1][:share_count].reshape(share_count * rows_each)
    slot_rows, slot_live = slot_plan(
        gathered[2][:share_count, 0],
        gathered[3][:share_count, 0],
        gathered[4][:share_count, 0],
        gathered[5][:share_count, 0],
        rows_each,
    )
    slot_rows = slot_rows + (jnp.arange(share_count, dtype=jnp.int32) * rows_each)[:, None, None]
    slot_rows = slot_rows.transpose(1, 0, 2).reshape(expert_count, -1)
    slot_live = slot_live.transpose(1, 0, 2).reshape(expert_count, -1)
    rows_in = features[slot_rows]
    scaling = weighting[slot_rows].astype(jnp.float32) * slot_live.astype(jnp.float32)
    gate_up = jnp.einsum(
        "erk,ekgh->ergh",
        rows_in,
        lax.all_gather(in_weights, "expert", axis=1, tiled=True),
        preferred_element_type=jnp.float32,
    )
    hidden_act = (jax.nn.silu(gate_up[:, :, 0]) * gate_up[:, :, 1] * scaling[:, :, None]).astype(
        jnp.bfloat16
    )
    token_total = share_count * rows_each
    expert_ids = jnp.arange(expert_count, dtype=jnp.int32)[:, None]
    placed = (
        jnp.zeros((expert_count, token_total, hidden_width), jnp.float32)
        .at[expert_ids, slot_rows]
        .add(hidden_act.astype(jnp.float32))
    )
    placed = (
        placed.transpose(1, 0, 2)
        .reshape(token_total, expert_count * hidden_width)
        .astype(jnp.bfloat16)
    )
    piece = lax.all_gather(out_weights, "expert", axis=2, tiled=True)
    flat_piece = piece.reshape(expert_count * hidden_width, piece.shape[2])
    partial_value = jnp.dot(placed, flat_piece, preferred_element_type=jnp.float32)
    rounded = partial_value.astype(jnp.bfloat16)
    terms = rounded.reshape(share_count, rows_each, tensor_count, local_cols)
    terms = terms.transpose(2, 0, 1, 3).reshape(tensor_count * share_count, rows_each, local_cols)
    summed = lax.psum_scatter(terms, ("tensor", "dp"), scatter_dimension=0, tiled=True).astype(
        jnp.float32
    )
    result = summed.reshape(rows_each, local_cols)
    return result.astype(jnp.bfloat16)


def solution(mesh):
    return jax.shard_map(
        local,
        mesh=mesh,
        in_specs=(
            P(("groups", "expert", "dp"), "tensor"),
            P(("groups", "expert", "dp")),
            P(("groups", "expert", "dp"), None),
            P(("groups", "expert", "dp"), None),
            P(("groups", "expert", "dp"), None, None),
            P(("groups", "expert", "dp"), None),
            P(None, "expert", None, ("tensor", "dp")),
            P(None, ("tensor", "dp"), "expert"),
        ),
        out_specs=P(("groups", "expert", "dp"), "tensor"),
        check_vma=False,
    )
```

profile of v0, /device:TPU:10, one launch (start us, length us, event | category | flops | bytes accessed | tf_op | source)
XLA Modules:
  0.0 837.8 jit_solution(15531366413804083286)
XLA Ops:
  6.5 0.0 all-gather.17.cloned.1.call-start
  6.5 0.7 all-gather.17.cloned.1.call-update
  7.3 0.0 all-gather.13.cloned.1.call-start
  7.3 7.3 copy.28
  14.6 0.0 copy-start.5
  14.6 0.0 copy-start.4
  14.6 0.0 all-gather.13.cloned.1.call-update
  14.7 0.0 all-gather.15.cloned.1.call-start
  14.7 0.7 all-gather.15.cloned.1.call-update
  15.4 0.0 reduce-scatter.2.cloned.1.call-start
  15.5 0.0 copy-done.1
  15.5 5.0 all-gather.6
  20.5 5.0 all-gather.8
  25.5 0.0 copy-done.3
  25.5 5.0 all-gather.7
  30.6 5.1 all-gather.1
  35.6 0.1 copy.25
  35.7 0.1 iota_add_fusion
  35.8 0.1 fusion.9
  35.9 0.1 reshape.71
  36.0 0.1 reshape.80
  36.1 0.6 dynamic-slice
  37.3 0.2 dynamic-update-slice
  37.6 6.3 all-reduce
  43.9 2.7 gather_fusion.1
  46.6 0.1 reshape.119
  46.7 0.1 copy.31
  46.8 0.1 copy.30
  46.8 0.1 iota_compare_fusion
  46.9 0.1 iota_compare_fusion.1
  47.0 0.1 add_bitcast_fusion
  47.1 0.1 reshape.74
  47.2 0.1 reshape.94
  47.3 5.7 copy.27
  52.9 0.3 copy.35
  53.3 6.5 gather_fusion
  59.7 468.4 %all-gather.13.cloned.1.call-done = bf16[2,7168,2,512]{3,1,2,0:T(8,128)(2,1)} async-done(((bf16[2,1792,2,512]{3,1,2,0:T(8,128)(2,1)}), bf16[2,7168,2,512]{3,1,2,0:T(8,128)(2,1)}) %all-gather.13.cloned.1.call-update) | async-done | bytes 29360144 | tf_op jit(solution)/shard_map/all_gather | solution.py:58
  528.1 14.9 %fusion.10 = f32[2,192,2,512]{3,1,2,0:T(8,128)S(1)} fusion(bf16[2,192,7168,1]{2,1,3,0:T(8,128)(2,1)} %bitcast.59, bf16[2,7168,2,512]{3,1,2,0:T(8,128)(2,1)} %all-gather.13.cloned.1.call-done), kind=kOutput, calls=%fused_computation.29 | convolution fusion | flops 5637144576 | bytes 36438016 | tf_op jit(solution)/shard_map/erk,ekgh->ergh/dot_general | solution.py:55
  543.0 0.3 fusion.3
  543.3 0.1 bitcast_convert_fusion
  543.4 0.1 broadcast_in_dim.16
  543.5 21.9 %scatter_fusion = f32[2,192,512]{2,1,0:T(8,128)S(1)} fusion(f32[2,192,512]{2,1,0:T(8,128)S(1)} %broadcast_in_dim.16, s32[384]{0:T(512)S(1)} %reshape.94, f32[384,512]{1,0:T(8,128)S(1)} %bitcast_convert_fusion), kind=kCustom, calls=%fused_computation.2 | custom fusion | flops 196608 | bytes 2362368 | tf_op jit(solution)/shard_map/scatter-add | solution.py:69
  565.5 215.0 %all-gather.15.cloned.1.call-done = bf16[2,512,7168]{2,1,0:T(8,128)(2,1)} async-done(((bf16[2,512,1792]{2,1,0:T(8,128)(2,1)}), bf16[2,512,7168]{2,1,0:T(8,128)(2,1)}) %all-gather.15.cloned.1.call-update) | async-done | bytes 14680080 | tf_op jit(solution)/shard_map/all_gather | solution.py:76
  780.4 8.2 fusion
  788.7 3.3 reshape.76
  791.9 3.7 copy.32
  795.6 0.0 reduce-scatter.2.cloned.1.call-update
  795.6 35.6 %reduce-scatter.2.cloned.1.call-done = bf16[1,96,3584]{2,1,0:T(8,128)(2,1)} async-done(((bf16[4,96,3584]{2,1,0:T(8,128)(2,1)}), bf16[1,96,3584]{2,1,0:T(8,128)(2,1)}) %reduce-scatter.2.cloned.1.call-update) | async-done | bytes 688144 | tf_op jit(solution)/shard_map/reduce_scatter | solution.py:82
  (20 shorter events, 0.1 us)
Async XLA Ops:
  6.5 40.7 %all-gather.17.cloned.1.call-start = ((), (), s32[]{:S(2)}) async-start(), calls=%async_computation.4 | async-start | bytes 3440640 | tf_op jit(solution)/shard_map/all_gather | solution.py:31
  7.3 520.9 %all-gather.13.cloned.1.call-start = ((), (), s32[]{:S(2)}) async-start(), calls=%async_computation.1 | async-start | bytes 36700160 | tf_op jit(solution)/shard_map/all_gather | solution.py:58
  14.6 0.8 copy-start.1
  14.6 5.9 copy-start.2
  14.6 10.9 %copy-start.3 = (s32[1,2]{1,0:T(1,128)S(1)}, s32[1,2]{1,0:T(1,128)}, u32[]{:S(2)}) copy-start(s32[1,2]{1,0:T(1,128)} %param.11) | copy-start | bytes 28
  14.6 16.0 %copy-start = (s32[1,2,32]{2,1,0:T(2,128)S(1)}, s32[1,2,32]{2,1,0:T(2,128)}, u32[]{:S(2)}) copy-start(s32[1,2,32]{2,1,0:T(2,128)} %param.12) | copy-start | bytes 772
  14.6 21.5 %copy-start.5 = (u32[32]{0:T(128)S(1)}, u32[32]{0:T(128)}, u32[]{:S(2)}) copy-start(u32[32]{0:T(128)} %constant.40) | copy-start | bytes 388
  14.6 22.7 %copy-start.4 = (bf16[96]{0:T(256)(128)(2,1)S(1)}, bf16[96]{0:T(256)(128)(2,1)}, u32[]{:S(2)}) copy-start(bf16[96]{0:T(256)(128)(2,1)} %param.9) | copy-start | bytes 580
  14.7 765.8 %all-gather.15.cloned.1.call-start = ((), (), s32[]{:S(2)}) async-start(), calls=%async_computation.2 | async-start | bytes 18350080 | tf_op jit(solution)/shard_map/all_gather | solution.py:76
  15.4 815.8 %reduce-scatter.2.cloned.1.call-start = ((), (), s32[]{:S(2)}) async-start(), calls=%async_computation.3 | async-start | bytes 3440640 | tf_op jit(solution)/shard_map/reduce_scatter | solution.py:82
Sparse Core Ops, SparseCore 0:
  8.9 26.5 all-gather.16
  37.1 491.0 all-gather.12
  529.7 250.6 all-gather.14
  795.8 35.4 reduce-scatter.1
where the time goes:
time: 841 us; the launch traced here: 838 us
  waiting for transfers between devices  720 us (86%)
  local copies, waits for them, and re-layouts  31.1 us (4%)
  blocking collectives  26.4 us (3%)
  matrix products  23.1 us (3%)
  other arithmetic  22.7 us (3%)
  between operations  13.9 us (2%)
    all_gather x1, waiting for transfers between devices, local(): lax.all_gather(in_weights, 'expert', axis=1, tiled=True)  468 us
    all_gather x1, waiting for transfers between devices, local(): piece = lax.all_gather(out_weights, 'expert', axis=2, tiled=True)  215 us
    reduce_scatter x1, waiting for transfers between devices, local(): lax.psum_scatter(terms, ('tensor', 'dp'), scatter_dimension=0, tiled=True)  35.6 us
    scatter-add x1, other arithmetic, local(): placed = jnp.zeros((expert_count, token_total, hidden_width), jnp.float32...  21.9 us
  transfers between devices with their start and end apart: 4, of which 3 were waited for; matrix products, arithmetic and copies ran while one was open for 7% of the time, Pallas kernels for 0%

commit v1 on v0

v1 whole, which is shorter than its diff:
```python
import jax
import jax.numpy as jnp
from jax import lax
from jax.sharding import PartitionSpec as P


def token_scales(route_weight, starts, counts, spills, spill_counts):
    rows_each = route_weight.shape[0]
    overflow = spills.shape[-1]
    capacity = rows_each - overflow
    first_pos = jnp.arange(capacity, dtype=jnp.int32)
    spill_pos = jnp.arange(overflow, dtype=jnp.int32)
    slot_rows = jnp.clip(
        jnp.concatenate([starts[:, None] + first_pos, spills], axis=-1), 0, rows_each - 1
    )
    slot_live = jnp.concatenate(
        [first_pos < counts[:, None], spill_pos < spill_counts[:, None]], axis=-1
    )
    hits = (slot_rows[:, :, None] == jnp.arange(rows_each)) & slot_live[:, :, None]
    live = jnp.sum(hits.astype(jnp.float32), axis=1)
    return live * route_weight.astype(jnp.float32)


def local(
    tokens, route_weight, block_start, block_count, spill_rows, spill_count, in_weights, out_weights
):
    rows, cols = tokens.shape
    n_z = lax.axis_size("expert")
    n_p = lax.axis_size("dp")
    depth = in_weights.shape[1]
    half = in_weights.shape[3]
    scales = token_scales(
        route_weight, block_start[0], block_count[0], spill_rows[0], spill_count[0]
    )
    scales_all = lax.all_gather(scales, ("expert", "dp"), axis=1, tiled=True)
    wide = lax.all_gather(tokens, "tensor", axis=1, tiled=True)
    wide = wide.reshape(rows, n_z, depth).transpose(1, 0, 2)
    mine = lax.all_to_all(wide, "expert", 0, 0, tiled=True)
    x = lax.all_gather(mine, "dp", axis=1, tiled=True).reshape(n_z * n_p * rows, depth)
    total = x.shape[0]
    use = (scales_all > 0).astype(x.dtype)
    part = sum(
        jnp.einsum(
            "rk,kgh->rgh", x * use[e][:, None], in_weights[e], preferred_element_type=jnp.float32
        )
        for e in range(2)
    )
    part = part.reshape(total, 2 * half).astype(jnp.bfloat16)
    gate_up = lax.psum_scatter(part, "expert", scatter_dimension=0, tiled=True).astype(jnp.float32)
    here = lax.all_gather(scales, "dp", axis=1, tiled=True)
    weight = jnp.sum(here, axis=0)
    act = (
        jax.nn.silu(gate_up[:, :half]) * gate_up[:, half:] * weight[:, None]
    ).astype(jnp.bfloat16)
    act = lax.all_gather(act, "expert", axis=0, tiled=True)
    placed = jnp.concatenate([act * use[0][:, None], act * use[1][:, None]], axis=1)
    out = jnp.dot(
        placed,
        out_weights.reshape(2 * half, depth),
        preferred_element_type=jnp.float32,
    ).astype(jnp.bfloat16)
    out = out.reshape(n_z, n_p, rows, depth).transpose(1, 0, 2, 3)
    out = lax.psum_scatter(out, "dp", scatter_dimension=0, tiled=True)[0]
    out = lax.all_to_all(out, "expert", 0, 0, tiled=True)
    out = out.transpose(1, 0, 2).reshape(rows, n_z * depth)
    return lax.psum_scatter(out, "tensor", scatter_dimension=1, tiled=True)


def solution(mesh):
    return jax.shard_map(
        local,
        mesh=mesh,
        in_specs=(
            P(("groups", "expert", "dp"), "tensor"),
            P(("groups", "expert", "dp")),
            P(("groups", "expert", "dp"), None),
            P(("groups", "expert", "dp"), None),
            P(("groups", "expert", "dp"), None, None),
            P(("groups", "expert", "dp"), None),
            P(None, "expert", None, ("tensor", "dp")),
            P(None, ("tensor", "dp"), "expert"),
        ),
        out_specs=P(("groups", "expert", "dp"), "tensor"),
        check_vma=False,
    )
```

time: 841 us -> 278 us (0.33)
  waiting for transfers between devices: 720 us -> 105 us
  blocking collectives: 26.4 us -> 102 us
  other arithmetic: 22.7 us -> 4.62 us
  matrix products: 23.1 us -> 10.4 us
  local copies, waits for them, and re-layouts: 31.1 us -> 39.6 us
    all_gather x3 -> x2, waiting for transfers between devices: 683 us -> 26.8 us  [the longest x1 26.8 us: local(): wide = lax.all_gather(tokens, 'tensor', axis=1, tiled=True)]
    all_to_all x0 -> x2, blocking collectives: none -> 72.6 us  [the longest x1 36.5 us: local(): out = lax.all_to_all(out, 'expert', 0, 0, tiled=True)]
    unnamed x4 -> x6, waiting for transfers between devices: 1.42 us -> 23.6 us
    scatter-add x1 -> x0, other arithmetic: 21.9 us -> none  [local(): placed = jnp.zeros((expert_count, token_total, hidden_width), jnp.float32...]
    reduce_scatter x1 -> x2, waiting for transfers between devices: 35.6 us -> 54.9 us  [the longest x1 31.6 us: local(): lax.psum_scatter(part, 'expert', scatter_dimension=0, tiled=True)]
    unnamed x17 -> x22, local copies, waits for them, and re-layouts: 8.5 us -> 23.1 us
    dot_general x2 -> x3, matrix products: 23.1 us -> 10.4 us  [the longest x2 6.12 us: local(): jnp.einsum('rk,kgh->rgh', x * use[e][:, None], in_weights[e], preferred_e...]
    gather x2 -> x0, local copies, waits for them, and re-layouts: 9.15 us -> none  [the longest x1 6.45 us: local(): rows_in = features[slot_rows]]
  transfers between devices with their start and end apart: 4 -> 5, of which waited for: 3 -> 4; matrix products, arithmetic and copies ran while one was open for 7% -> 11% of each run, Pallas kernels for 0% -> 0%
where the time goes in v1:
time: 278 us; the launch traced here: 275 us
  waiting for transfers between devices  105 us (38%)
  blocking collectives  102 us (37%)
  local copies, waits for them, and re-layouts  39.6 us (14%)
  between operations  13.3 us (5%)
  matrix products  10.4 us (4%)
  other arithmetic  4.62 us (2%)
    all_to_all x1, blocking collectives, local(): out = lax.all_to_all(out, 'expert', 0, 0, tiled=True)  36.5 us
    all_to_all x1, blocking collectives, local(): mine = lax.all_to_all(wide, 'expert', 0, 0, tiled=True)  36 us
    reduce_scatter x1, waiting for transfers between devices, local(): lax.psum_scatter(part, 'expert', scatter_dimension=0, tiled=True)  31.6 us
    all_gather x1, waiting for transfers between devices, local(): wide = lax.all_gather(tokens, 'tensor', axis=1, tiled=True)  26.8 us
    unnamed x6, waiting for transfers between devices  23.6 us
    reduce_scatter x1, waiting for transfers between devices, local(): return lax.psum_scatter(out, 'tensor', scatter_dimension=1, tiled=True)  23.3 us
    unnamed x22, local copies, waits for them, and re-layouts  23.1 us
    all_gather x1, blocking collectives, local(): act = lax.all_gather(act, 'expert', axis=0, tiled=True)  17.4 us
  transfers between devices with their start and end apart: 5, of which 4 were waited for; matrix products, arithmetic and copies ran while one was open for 11% of the time, Pallas kernels for 0%

profile of v1, /device:TPU:10, one launch (start us, length us, event | category | flops | bytes accessed | tf_op | source)
XLA Modules:
  0.0 275.1 jit_solution(727283088759707055)
XLA Ops:
  6.5 0.7 all-gather.5.cloned.1.call-update
  7.3 0.0 all-gather.7.cloned.1.call-start
  7.3 26.8 %all-gather.5.cloned.1.call-done = bf16[96,7168]{1,0:T(8,128)(2,1)} async-done(((bf16[96,3584]{1,0:T(8,128)(2,1)}), bf16[96,7168]{1,0:T(8,128)(2,1)}) %all-gather.5.cloned.1.call-update) | async-done | bytes 1376272 | tf_op jit(solution)/shard_map/all_gather | solution.py:36
  34.2 2.9 %reshape.61 = bf16[96,4,1792]{2,1,0:T(4,128)(2,1)S(1)} reshape(bf16[96,7168]{1,0:T(8,128)(2,1)} %all-gather.5.cloned.1.call-done) | data formatting | bytes 2752512 | tf_op jit(solution)/shard_map/reshape | solution.py:37
  37.1 0.1 copy.46
  37.3 36.0 %all_to_all.10 = bf16[4,96,1792]{2,1,0:T(8,128)(2,1)S(1)} all-to-all(bf16[4,96,1792]{2,1,0:T(8,128)(2,1)S(1)} %copy.46), channel_id=1, replica_groups=mesh['groups'=2,'expert'=4,'tensor'=2,'dp'=2] {'expert'}, dimensions={0} | all-to-all | bytes 2752512 | tf_op jit(solution)/shard_map/all_to_all | solution.py:38
  73.3 0.0 copy-start.2
  73.3 2.2 copy.47
  75.5 0.0 all-gather.7.cloned.1.call-update
  75.5 0.0 reduce-scatter.10.cloned.1.call-start
  75.6 0.1 iota_compare_fusion.1
  75.7 0.1 iota_compare_fusion.2
  75.7 0.1 pad_add_fusion
  75.8 0.1 iota_add_fusion
  75.9 0.1 add_clamp_fusion
  76.0 0.1 convert_reduce_fusion
  76.1 10.0 %all-gather = f32[8,96,2]{1,2,0:T(2,128)S(1)} all-gather(f32[1,96,2]{1,2,0:T(2,128)S(1)} %multiply_bitcast_fusion), channel_id=1, replica_groups=mesh['groups'=2,'expert'=4,'tensor'=2,'dp'=2] {'expert','dp'}, dimensions={0}, use_global_device_ids=true | all-gather | bytes 6912 | tf_op jit(solution)/shard_map/all_gather | solution.py:35
  86.1 0.1 reshape.72
  86.3 0.1 mul.71
  86.3 0.1 mul.75
  86.4 7.6 %fusion.14 = (bf16[1,1792,2,512]{3,2,1,0:T(2,128)(2,1)}, bf16[1,1792,2,512]{3,2,1,0:T(2,128)(2,1)}) fusion(bf16[2,1792,2,512]{3,2,1,0:T(2,128)(2,1)} %param.14), kind=kLoop, calls=%fused_computation.31 | loop fusion | bytes 14680064 | tf_op jit(solution)/shard_map/slice | solution.py:44
  94.1 9.9 %copy.60 = bf16[1,1792,2,512]{1,3,2,0:T(8,128)(2,1)} copy(bf16[1,1792,2,512]{3,2,1,0:T(2,128)(2,1)} %get-tuple-element.8) | data formatting | bytes 7340032
  103.9 9.9 %copy.59 = bf16[1,1792,2,512]{1,3,2,0:T(8,128)(2,1)} copy(bf16[1,1792,2,512]{3,2,1,0:T(2,128)(2,1)} %get-tuple-element.7) | data formatting | bytes 7340032
  113.9 2.5 copy_multiply_fusion.1
  116.3 0.4 copy-done.1
  116.7 3.0 %fusion = f32[768,2,512]{0,2,1:T(8,128)S(1)} fusion(bf16[768,1792,1]{1,0,2:T(8,128)(2,1)S(1)} %bitcast.51, bf16[1,1792,2,512]{1,3,2,0:T(8,128)(2,1)S(1)} %copy-done.1), kind=kOutput, calls=%fused_computation | convolution fusion | flops 2818572288 | bytes 9568256 | tf_op jit(solution)/shard_map/rk,kgh->rgh/dot_general | solution.py:43
  119.8 3.1 %add_convert_fusion = bf16[768,2,512]{0,2,1:T(8,128)(2,1)S(1)} fusion(f32[768,2,512]{0,2,1:T(8,128)S(1)} %fusion, bf16[768,1792,1]{1,0,2:T(8,128)(2,1)S(1)} %bitcast.50, bf16[1,1792,2,512]{1,3,2,0:T(8,128)(2,1)S(1)} %copy-done), kind=kOutput, calls=%fused_computation.5 | convolution fusion | flops 2820145152 | bytes 11141120 | tf_op jit(solution)/shard_map/rk,kgh->rgh/dot_general | solution.py:43
  122.9 1.6 copy.55
  124.5 0.0 reduce-scatter.10.cloned.1.call-update
  124.6 0.0 all-reduce.3.cloned.1.call-start
  124.6 1.8 all-gather.1
  126.4 0.1 reshape.69
  126.5 31.6 %reduce-scatter.10.cloned.1.call-done = bf16[192,1024]{1,0:T(8,128)(2,1)} async-done(((bf16[768,1024]{1,0:T(8,128)(2,1)}), bf16[192,1024]{1,0:T(8,128)(2,1)}) %reduce-scatter.10.cloned.1.call-update) | async-done | bytes 393232 | tf_op jit(solution)/shard_map/reduce_scatter | solution.py:49
  158.1 1.2 convert_element_type.29
  159.4 0.1 fusion.10
  159.5 17.4 %all_gather.19 = bf16[768,512]{1,0:T(8,128)(2,1)S(1)} all-gather(bf16[192,512]{1,0:T(8,128)(2,1)S(1)} %fusion.10), channel_id=1, replica_groups=mesh['groups'=2,'expert'=4,'tensor'=2,'dp'=2] {'expert'}, dimensions={0}, use_global_device_ids=true | all-gather | bytes 983040 | tf_op jit(solution)/shard_map/all_gather | solution.py:55
  176.9 0.3 broadcast_multiply_fusion.1
  177.2 4.3 %convolution_convert_fusion = bf16[768,1792]{1,0:T(8,128)(2,1)} fusion(bf16[1024,1792]{1,0:T(8,128)(2,1)S(1)} %bitcast.56, bf16[768,512]{1,0:T(8,128)(2,1)S(1)} %get-tuple-element.12, bf16[768,512]{1,0:T(8,128)(2,1)S(1)} %get-tuple-element.11), kind=kOutput, calls=%fused_computation.4 | convolution fusion | flops 2823094272 | bytes 7995392 | tf_op jit(solution)/shard_map/dot_general | solution.py:57
  181.4 0.0 all-reduce.3.cloned.1.call-update
  181.5 0.0 reduce-scatter.8.cloned.1.call-start
  181.5 0.6 copy-done.8
  182.1 0.6 dynamic-slice
  182.7 22.8 %all-reduce.3.cloned.1.call-done = bf16[2,4,96,1792]{3,2,0,1:T(8,128)(2,1)} async-done(((bf16[2,4,96,1792]{3,2,0,1:T(8,128)(2,1)}), bf16[2,4,96,1792]{3,2,0,1:T(8,128)(2,1)}) %all-reduce.3.cloned.1.call-update) | async-done | bytes 2752528
  205.5 2.1 dynamic-slice_bitcast_fusion
  207.5 36.5 %all_to_all.11 = bf16[4,96,1792]{2,1,0:T(8,128)(2,1)S(1)} all-to-all(bf16[4,96,1792]{2,1,0:T(8,128)(2,1)S(1)} %dynamic-slice_bitcast_fusion), channel_id=1, replica_groups=mesh['groups'=2,'expert'=4,'tensor'=2,'dp'=2] {'expert'}, dimensions={0} | all-to-all | bytes 2752512 | tf_op jit(solution)/shard_map/all_to_all | solution.py:64
  244.1 1.2 copy.61
  245.3 0.0 reduce-scatter.8.cloned.1.call-update
  245.3 23.3 %reduce-scatter.8.cloned.1.call-done = bf16[96,3584]{1,0:T(8,128)(2,1)} async-done(((bf16[96,7168]{1,0:T(8,128)(2,1)}), bf16[96,3584]{1,0:T(8,128)(2,1)}) %reduce-scatter.8.cloned.1.call-update) | async-done | bytes 688144 | tf_op jit(solution)/shard_map/reduce_scatter | solution.py:66
  (22 shorter events, 0.1 us)
Async XLA Ops:
  6.5 27.6 %all-gather.5.cloned.1.call-start = ((), (), s32[]{:S(2)}) async-start(), calls=%async_computation.4 | async-start | bytes 2064384 | tf_op jit(solution)/shard_map/all_gather | solution.py:36
  7.3 106.6 %all-gather.7.cloned.1.call-start = ((), (), s32[]{:S(2)}) async-start(), calls=%async_computation.5 | async-start | bytes 4128768 | tf_op jit(solution)/shard_map/all_gather | solution.py:39
  73.3 2.3 copy-start.4
  73.3 2.3 copy-start.5
  73.3 2.4 copy-start.6
  73.3 2.5 copy-start.7
  73.3 2.6 copy-start.2
  75.5 82.6 %reduce-scatter.10.cloned.1.call-start = ((), (), s32[]{:S(2)}) async-start(), calls=%async_computation.7 | async-start | bytes 1966080 | tf_op jit(solution)/shard_map/reduce_scatter | solution.py:49
  113.9 2.9 %copy-start.1 = (bf16[1,1792,2,512]{1,3,2,0:T(8,128)(2,1)S(1)}, bf16[1,1792,2,512]{1,3,2,0:T(8,128)(2,1)}, u32[]{:S(2)}) copy-start(bf16[1,1792,2,512]{1,3,2,0:T(8,128)(2,1)} %copy.60) | copy-start | bytes 11010052
  116.7 3.0 %copy-start = (bf16[1,1792,2,512]{1,3,2,0:T(8,128)(2,1)S(1)}, bf16[1,1792,2,512]{1,3,2,0:T(8,128)(2,1)}, u32[]{:S(2)}) copy-start(bf16[1,1792,2,512]{1,3,2,0:T(8,128)(2,1)} %copy.59) | copy-start | bytes 11010052
  124.6 80.9 %all-reduce.3.cloned.1.call-start = ((), (), s32[]{:S(2)}) async-start(), calls=%async_computation.8 | async-start | bytes 5505024
  158.1 19.0 %copy-start.3 = (bf16[2,512,1792]{2,1,0:T(8,128)(2,1)S(1)}, bf16[2,512,1792]{2,1,0:T(8,128)(2,1)}, u32[]{:S(2)}) copy-start(bf16[2,512,1792]{2,1,0:T(8,128)(2,1)} %param.15) | copy-start | bytes 11010052
  181.4 0.7 copy-start.8
  181.5 87.1 %reduce-scatter.8.cloned.1.call-start = ((), (), s32[]{:S(2)}) async-start(), calls=%async_computation.6 | async-start | bytes 2064384 | tf_op jit(solution)/shard_map/reduce_scatter | solution.py:66
Sparse Core Ops, SparseCore 0:
  8.9 25.2 all-gather.4
  75.6 11.9 all-gather.6
  124.7 33.4 reduce-scatter.9
  181.6 23.8 all-reduce.2
  245.4 23.1 reduce-scatter.7

commit v2 on v1

v2 whole, which is shorter than its diff:
```python
import functools

import jax
import jax.numpy as jnp
from jax import lax
from jax.experimental import pallas as pl
from jax.experimental.pallas import tpu as pltpu
from jax.sharding import PartitionSpec as P

MESH = pl.DeviceIdType.MESH
LANES = 128


def token_scales(route_weight, starts, counts, spills, spill_counts):
    rows_each = route_weight.shape[0]
    overflow = spills.shape[-1]
    capacity = rows_each - overflow
    first_pos = jnp.arange(capacity, dtype=jnp.int32)
    spill_pos = jnp.arange(overflow, dtype=jnp.int32)
    slot_rows = jnp.clip(
        jnp.concatenate([starts[:, None] + first_pos, spills], axis=-1), 0, rows_each - 1
    )
    slot_live = jnp.concatenate(
        [first_pos < counts[:, None], spill_pos < spill_counts[:, None]], axis=-1
    )
    hits = (slot_rows[:, :, None] == jnp.arange(rows_each)) & slot_live[:, :, None]
    live = jnp.sum(hits.astype(jnp.float32), axis=1)
    return live * route_weight.astype(jnp.float32)


def kernel(
    n_t, n_z, n_r, rows, width, half,
    xs, w_in, w_out, out_ref,
    wi, wo, first, x_all, part, part_in, hid, o_both, o_sib, x_out, x_in, z_out, z_in, last,
    wsem, lsem, s0, r0, s1, r1, s2, r2, s3, r3, s4, r4, s5, r5, s6, r6, s7, r7, s8, r8, s9, r9,
):
    e = lax.axis_index("expert")
    t = lax.axis_index("tensor")
    p = lax.axis_index("dp")
    other = 1 - p
    total = 2 * n_t * rows

    load_in = pltpu.make_async_copy(w_in, wi, wsem.at[0])
    load_out = pltpu.make_async_copy(w_out, wo, wsem.at[1])
    own_piece = pltpu.make_async_copy(xs.at[t], first.at[t], lsem.at[0])
    own_piece.start()
    load_in.start()
    load_out.start()

    barrier = pltpu.get_barrier_semaphore()
    for k in range(1, n_t):
        pl.semaphore_signal(
            barrier, inc=1, device_id={"tensor": lax.rem(t + k, n_t)}, device_id_type=MESH
        )
    for k in range(1, n_z):
        pl.semaphore_signal(
            barrier, inc=1, device_id={"expert": lax.rem(e + k, n_z)}, device_id_type=MESH
        )
    pl.semaphore_signal(barrier, inc=1, device_id={"dp": other}, device_id_type=MESH)
    pl.semaphore_wait(barrier, n_t + n_z - 1)

    def remote(src, dst, send, recv, **where):
        return pltpu.make_async_remote_copy(
            src_ref=src,
            dst_ref=dst,
            send_sem=send,
            recv_sem=recv,
            device_id=where,
            device_id_type=MESH,
        )

    def spread(to, j, came):
        return remote(
            xs.at[to, j], first.at[came, j], s0.at[to, j], r0.at[came, j], tensor=to
        )

    def across(block, to, came):
        return remote(
            first.at[block // n_r, lax.rem(block, n_r)],
            x_all.at[came, p, t],
            s1.at[to],
            r1.at[came],
            expert=to,
        )

    def widen(block, to, came):
        return remote(
            x_all.at[block, p, came],
            x_all.at[block, p, came],
            s2.at[block, to],
            r2.at[block, came],
            tensor=to,
        )

    def pair(block, core):
        return remote(
            x_all.at[block, core], x_all.at[block, core], s3.at[block], r3.at[block], dp=other
        )

    def partial(block, came):
        return remote(part.at[block], part_in.at[came], s4.at[block], r4.at[came], expert=block)

    def hidden(to, came):
        return remote(hid.at[came], hid.at[came], s5.at[to], r5.at[came], expert=to)

    def sibling(block):
        return remote(
            o_both.at[block, other], o_sib.at[block], s6.at[block], r6.at[block], dp=other
        )

    def reduce_x(block, to, came):
        return remote(
            x_out.at[block, to], x_in.at[block, came], s7.at[block, to], r7.at[block, came],
            tensor=to,
        )

    def deliver(to, came):
        return remote(z_out.at[to], z_in.at[came], s8.at[to], r8.at[came], expert=to)

    def finish(block, to, j, came):
        return remote(
            z_in.at[block], last.at[j, came], s9.at[block], r9.at[j, came], tensor=to
        )

    for j in range(n_r):
        for k in range(1, n_t):
            spread(lax.rem(t + k, n_t), j, t).start()
    own_piece.wait()
    for k in range(n_t):
        ts = lax.rem(t + k, n_t)
        for j in range(n_r):
            block = ts * n_r + j
            if k > 0:
                spread(ts, j, ts).wait_recv()

            @pl.when(block != e)
            def _():
                across(block, block, e).start()

            @pl.when(block == e)
            def _():
                pltpu.make_async_copy(first.at[ts, j], x_all.at[e, p, t], lsem.at[1]).start()

    def stage_a(k):
        es = lax.rem(e + k, n_z)
        if k == 0:
            pltpu.make_async_copy(first.at[0, 0], x_all.at[e, p, t], lsem.at[1]).wait()
        else:
            across(es, es, es).wait_recv()
        for i in range(1, n_t):
            widen(es, lax.rem(t + i, n_t), t).start()

    def stage_b(k):
        es = lax.rem(e + k, n_z)
        for i in range(1, n_t):
            ts = lax.rem(t + i, n_t)
            widen(es, ts, ts).wait_recv()
        pair(es, p).start()

    def signs(es):
        meta = x_all[es, :, :, :, :LANES].reshape(total, LANES)
        return meta.astype(jnp.float32)[:, :1]

    tile = min(half, 256)
    tiles = half // tile

    def stage_c(k):
        es = lax.rem(e + k, n_z)
        pair(es, other).wait_recv()
        second = signs(es) < 0

        def step(i, carry):
            g = i // tiles
            cols = pl.ds(pl.multiple_of(lax.rem(i, tiles) * tile, tile), tile)
            x = x_all[es, :, :, :, LANES:].reshape(total, width)
            zero = jnp.dot(x, wi[0, g, :, cols], preferred_element_type=jnp.float32)
            one = jnp.dot(x, wi[1, g, :, cols], preferred_element_type=jnp.float32)
            value = jnp.where(second, one, zero).astype(jnp.bfloat16)
            if k == 0:
                part_in[e, g, :, cols] = value
            else:
                part[es, g, :, cols] = value
            return carry

        lax.fori_loop(0, 2 * tiles, step, 0)
        if k > 0:
            partial(es, e).start()

    for step in range(n_z + 2):
        if step < n_z:
            stage_a(step)
        if 0 <= step - 1 < n_z:
            stage_b(step - 1)
        if step - 1 == 0:
            load_in.wait()
        if 0 <= step - 2 < n_z:
            stage_c(step - 2)

    for k in range(1, n_z):
        es = lax.rem(e + k, n_z)
        partial(es, es).wait_recv()
    gate = jnp.zeros((total, half), jnp.float32)
    up = jnp.zeros((total, half), jnp.float32)
    for k in range(n_z):
        gate = gate + part_in[k, 0].astype(jnp.float32)
        up = up + part_in[k, 1].astype(jnp.float32)
    act = gate / (1.0 + jnp.exp(-gate)) * up * jnp.abs(signs(e))
    hid[e] = act.astype(jnp.bfloat16)
    for k in range(1, n_z):
        hidden(lax.rem(e + k, n_z), e).start()

    load_out.wait()
    wide = 256 if width % 256 == 0 else width

    def stage_d(k):
        es = lax.rem(e + k, n_z)
        if k > 0:
            hidden(es, es).wait_recv()
        second = signs(es) < 0
        h = hid[es].astype(jnp.float32)
        h0 = jnp.where(second, 0.0, h).astype(jnp.bfloat16)
        h1 = jnp.where(second, h, 0.0).astype(jnp.bfloat16)

        def column(i):
            if wide == width:
                cols = slice(None)
            else:
                cols = pl.ds(pl.multiple_of(i * wide, wide), wide)
            value = jnp.dot(h0, wo[0, :, cols], preferred_element_type=jnp.float32)
            value = value + jnp.dot(h1, wo[1, :, cols], preferred_element_type=jnp.float32)
            value = value.astype(jnp.bfloat16).reshape(2, n_t, rows, wide)
            o_both[es, :, :, :, cols] = value

        if wide == width:
            column(0)
        else:
            lax.fori_loop(0, width // wide, lambda i, c: (column(i), c)[1], 0)
        sibling(es).start()

    def stage_e(k):
        es = lax.rem(e + k, n_z)
        sibling(es).wait_recv()
        both = o_both[es, p].astype(jnp.float32) + o_sib[es].astype(jnp.float32)
        x_out[es] = both.astype(jnp.bfloat16)
        for i in range(1, n_t):
            reduce_x(es, lax.rem(t + i, n_t), t).start()

    def stage_f(k):
        es = lax.rem(e + k, n_z)
        value = x_out[es, t].astype(jnp.float32)
        for i in range(1, n_t):
            ts = lax.rem(t + i, n_t)
            reduce_x(es, ts, ts).wait_recv()
            value = value + x_in[es, ts].astype(jnp.float32)
        if k == 0:
            z_in[e] = value.astype(jnp.bfloat16)
        else:
            z_out[es] = value.astype(jnp.bfloat16)
            deliver(es, e).start()

    for step in range(n_z + 2):
        if step < n_z:
            stage_d(step)
        if 0 <= step - 1 < n_z:
            stage_e(step - 1)
        if 0 <= step - 2 < n_z:
            stage_f(step - 2)

    for k in range(n_z):
        es = lax.rem(e + k, n_z)
        if k > 0:
            deliver(es, es).wait_recv()
        owner = es // n_r
        j = lax.rem(es, n_r)

        @pl.when(owner != t)
        def _():
            finish(es, owner, j, t).start()

        @pl.when(owner == t)
        def _():
            last[j, t] = z_in[es]

    for k in range(1, n_t):
        ts = lax.rem(t + k, n_t)
        for j in range(n_r):
            finish(0, ts, j, ts).wait_recv()
    out_ref[...] = last[...]

    for k in range(1, n_t):
        ts = lax.rem(t + k, n_t)
        for j in range(n_r):
            spread(ts, j, t).wait_send()
            finish(ts * n_r + j, ts, j, t).wait_send()
        for b in range(n_z):
            widen(b, ts, t).wait_send()
            reduce_x(b, ts, t).wait_send()
    for k in range(1, n_z):
        es = lax.rem(e + k, n_z)
        across(es, es, e).wait_send()
        partial(es, e).wait_send()
        hidden(es, e).wait_send()
        deliver(es, e).wait_send()
    for b in range(n_z):
        pair(b, p).wait_send()
        sibling(b).wait_send()


def local(
    tokens, route_weight, block_start, block_count, spill_rows, spill_count, in_weights, out_weights
):
    rows_each, cols = tokens.shape
    n_z = lax.axis_size("expert")
    n_t = lax.axis_size("tensor")
    n_r = n_z // n_t
    width = in_weights.shape[1]
    half = in_weights.shape[3]
    scales = token_scales(
        route_weight, block_start[0], block_count[0], spill_rows[0], spill_count[0]
    )
    signed = (scales[0] - scales[1]).astype(jnp.bfloat16)
    rows = -(-rows_each // (16 * n_t)) * 16
    extra = rows * n_t - rows_each
    if extra:
        tokens = jnp.pad(tokens, ((0, extra), (0, 0)))
        signed = jnp.pad(signed, (0, extra))
    meta = jnp.broadcast_to(signed.reshape(n_t, 1, rows, 1), (n_t, n_r, rows, LANES))
    blocks = tokens.reshape(n_t, rows, n_r, width).transpose(0, 2, 1, 3)
    xs = jnp.concatenate([meta, blocks], axis=-1)
    w_in = in_weights.transpose(0, 2, 1, 3)

    total = 2 * n_t * rows
    long = width + LANES
    b16 = jnp.bfloat16
    dma = pltpu.SemaphoreType.DMA
    sems = [
        dma((2,)), dma((2,)),
        dma((n_t, n_r)), dma((n_t, n_r)),
        dma((n_z,)), dma((n_z,)),
        dma((n_z, n_t)), dma((n_z, n_t)),
        dma((n_z,)), dma((n_z,)),
        dma((n_z,)), dma((n_z,)),
        dma((n_z,)), dma((n_z,)),
        dma((n_z,)), dma((n_z,)),
        dma((n_z, n_t)), dma((n_z, n_t)),
        dma((n_z,)), dma((n_z,)),
        dma((n_z,)), dma((n_r, n_t)),
    ]
    vmem = pltpu.VMEM
    out = pl.pallas_call(
        functools.partial(kernel, n_t, n_z, n_r, rows, width, half),
        out_shape=jax.ShapeDtypeStruct((n_r, n_t, rows, width), b16),
        in_specs=[
            pl.BlockSpec(memory_space=pltpu.VMEM),
            pl.BlockSpec(memory_space=pl.ANY),
            pl.BlockSpec(memory_space=pl.ANY),
        ],
        out_specs=pl.BlockSpec(memory_space=pltpu.VMEM),
        scratch_shapes=[
            vmem(w_in.shape, b16),
            vmem(out_weights.shape, b16),
            vmem((n_t, n_r, rows, long), b16),
            vmem((n_z, 2, n_t, rows, long), b16),
            vmem((n_z, 2, total, half), b16),
            vmem((n_z, 2, total, half), b16),
            vmem((n_z, total, half), b16),
            vmem((n_z, 2, n_t, rows, width), b16),
            vmem((n_z, n_t, rows, width), b16),
            vmem((n_z, n_t, rows, width), b16),
            vmem((n_z, n_t, rows, width), b16),
            vmem((n_z, rows, width), b16),
            vmem((n_z, rows, width), b16),
            vmem((n_r, n_t, rows, width), b16),
        ] + sems,
        compiler_params=pltpu.CompilerParams(
            collective_id=0, has_side_effects=True, vmem_limit_bytes=56 * 1024 * 1024
        ),
    )(xs, w_in, out_weights)
    out = out.transpose(1, 2, 0, 3).reshape(n_t * rows, cols)
    return out[:rows_each]


def solution(mesh):
    return jax.shard_map(
        local,
        mesh=mesh,
        in_specs=(
            P(("groups", "expert", "dp"), "tensor"),
            P(("groups", "expert", "dp")),
            P(("groups", "expert", "dp"), None),
            P(("groups", "expert", "dp"), None),
            P(("groups", "expert", "dp"), None, None),
            P(("groups", "expert", "dp"), None),
            P(None, "expert", None, ("tensor", "dp")),
            P(None, ("tensor", "dp"), "expert"),
        ),
        out_specs=P(("groups", "expert", "dp"), "tensor"),
        check_vma=False,
    )
```

time: 278 us -> 143 us (0.51)
  Pallas kernels: 0 us -> 125 us
  waiting for transfers between devices: 105 us -> 0 us
  blocking collectives: 102 us -> 0 us
  local copies, waits for them, and re-layouts: 39.6 us -> 12.4 us
  between operations: 13.3 us -> 0.05 us
  matrix products: 10.4 us -> 0 us
    pallas_call x0 -> x1, Pallas kernels: none -> 125 us  [local(): pl.pallas_call(functools.partial(kernel, n_t, n_z, n_r, rows, width, half...]
    all_to_all x2 -> x0, blocking collectives: 72.6 us -> none  [the longest x1 36.5 us: local(): out = lax.all_to_all(out, 'expert', 0, 0, tiled=True)]
    reduce_scatter x2 -> x0, waiting for transfers between devices: 54.9 us -> none  [the longest x1 31.6 us: local(): lax.psum_scatter(part, 'expert', scatter_dimension=0, tiled=True)]
    all_gather x3 -> x0, blocking collectives: 29.2 us -> none  [the longest x1 17.4 us: local(): act = lax.all_gather(act, 'expert', axis=0, tiled=True)]
    all_gather x2 -> x0, waiting for transfers between devices: 26.8 us -> none  [the longest x1 26.8 us: local(): wide = lax.all_gather(tokens, 'tensor', axis=1, tiled=True)]
    unnamed x6 -> x0, waiting for transfers between devices: 23.6 us -> none
    unnamed x22 -> x2, local copies, waits for them, and re-layouts: 23.1 us -> 8.2 us
    dot_general x3 -> x0, matrix products: 10.4 us -> none  [the longest x2 6.12 us: local(): jnp.einsum('rk,kgh->rgh', x * use[e][:, None], in_weights[e], preferred_e...]
  transfers between devices with their start and end apart: 5 -> 0, of which waited for: 4 -> 0; matrix products, arithmetic and copies ran while one was open for 11% -> 0% of each run, Pallas kernels for 0% -> 0%
where the time goes in v2:
time: 143 us
  Pallas kernels  125 us (87%)
  local copies, waits for them, and re-layouts  12.4 us (9%)
  other arithmetic  4.74 us (3%)
    pallas_call x1, Pallas kernels, local(): pl.pallas_call(functools.partial(kernel, n_t, n_z, n_r, rows, width, half...  125 us
    unnamed x2, local copies, waits for them, and re-layouts  8.2 us

profile of v2, /device:TPU:10, one launch (start us, length us, event | category | flops | bytes accessed | tf_op | source)
XLA Modules:
  0.0 142.6 jit_solution(8669112936833875145)
XLA Ops:
  0.0 0.7 convert_element_type.17
  0.7 0.7 iota_compare_fusion.2
  1.4 0.7 iota_compare_fusion.1
  2.1 0.1 pad_add_fusion
  2.2 0.7 iota_add_fusion
  2.9 0.8 add_clamp_fusion
  3.7 0.1 convert_reduce_fusion
  3.8 0.1 convert_element_type.19
  3.9 0.1 broadcast_in_dim.2
  4.0 2.1 %reshape.50 = bf16[2,48,2,1792]{3,2,1,0:T(2,128)(2,1)S(1)} reshape(bf16[96,3584]{1,0:T(8,128)(2,1)} %param.8) | data formatting | bytes 1376256 | tf_op jit(solution)/shard_map/reshape | solution.py:328
  6.2 0.1 copy.20
  6.2 0.9 pad_maximum_fusion.xs
  7.2 7.3 %copy.19 = bf16[2,1792,2,512]{3,1,2,0:T(8,128)(2,1)} copy(bf16[2,1792,2,512]{3,2,1,0:T(2,128)(2,1)} %param.14) | data formatting | bytes 14680064 | tf_op args[6]
  14.4 125.5 %shard_map.82 = bf16[2,2,48,1792]{3,2,1,0:T(8,128)(2,1)} custom-call(bf16[2,2,48,1920]{3,2,1,0:T(8,128)(2,1)} %pad_maximum_fusion.xs, bf16[2,2,1792,512]{3,2,1,0:T(8,128)(2,1)} %bitcast.14, bf16[2,512,1792]{2,1,0:T(8,128)(2,1)} %w_out.1), custom_call_target="tpu_custom_call" | custom-call | tf_op jit(solution)/shard_map/pallas_call | solution.py:350
  139.9 1.8 %copy.15 = bf16[2,48,2,1792]{3,2,1,0:T(2,128)(2,1)S(1)} copy(bf16[2,48,2,1792]{3,1,0,2:T(8,128)(2,1)} %bitcast.17) | data formatting | bytes 1376256 | tf_op jit(solution)/shard_map/transpose | solution.py:379
  141.7 0.9 copy.16
  (2 shorter events, 0.0 us)

commit v3 on v2

--- a/solution.py
+++ b/solution.py
@@ -31,7 +31,7 @@
 def kernel(
     n_t, n_z, n_r, rows, width, half,
     xs, w_in, w_out, out_ref,
-    wi, wo, first, x_all, part, part_in, hid, o_both, o_sib, x_out, x_in, z_out, z_in, last,
+    wi, wo, first, x_all, part, run_out, run_in, hid, o_both, o_sib, x_out, x_in, z_out, z_in, last,
     wsem, lsem, s0, r0, s1, r1, s2, r2, s3, r3, s4, r4, s5, r5, s6, r6, s7, r7, s8, r8, s9, r9,
 ):
     e = lax.axis_index("expert")
@@ -97,11 +97,22 @@
             x_all.at[block, core], x_all.at[block, core], s3.at[block], r3.at[block], dp=other
         )
 
-    def partial(block, came):
-        return remote(part.at[block], part_in.at[came], s4.at[block], r4.at[came], expert=block)
-
-    def hidden(to, came):
-        return remote(hid.at[came], hid.at[came], s5.at[to], r5.at[came], expert=to)
+    def partial(block, c, to):
+        return remote(
+            run_out.at[block, c], run_in.at[block, c], s4.at[block, c], r4.at[block, c], expert=to
+        )
+
+    def hidden(block, c, to):
+        return remote(
+            hid.at[block, c], hid.at[block, c], s5.at[block, c], r5.at[block, c], expert=to
+        )
+
+    last_z = n_z - 1
+    order = []
+    for i in range(n_z // 2):
+        order += [(last_z - i, True), (i, False)]
+    prev_z = jnp.maximum(e - 1, 0)
+    next_z = jnp.minimum(e + 1, last_z)
 
     def sibling(block):
         return remote(
@@ -175,16 +186,22 @@
             x = x_all[es, :, :, :, LANES:].reshape(total, width)
             zero = jnp.dot(x, wi[0, g, :, cols], preferred_element_type=jnp.float32)
             one = jnp.dot(x, wi[1, g, :, cols], preferred_element_type=jnp.float32)
-            value = jnp.where(second, one, zero).astype(jnp.bfloat16)
-            if k == 0:
-                part_in[e, g, :, cols] = value
-            else:
-                part[es, g, :, cols] = value
+            part[es, i] = jnp.where(second, one, zero)
             return carry
 
         lax.fori_loop(0, 2 * tiles, step, 0)
-        if k > 0:
-            partial(es, e).start()
+
+        @pl.when((e == last_z) & (es >= n_z // 2))
+        def _():
+            for c in range(2 * tiles):
+                run_out[es, c] = part[es, c].astype(jnp.bfloat16)
+                partial(es, c, prev_z).start()
+
+        @pl.when((e == 0) & (es < n_z // 2))
+        def _():
+            for c in range(2 * tiles):
+                run_out[es, c] = part[es, c].astype(jnp.bfloat16)
+                partial(es, c, next_z).start()
 
     for step in range(n_z + 2):
         if step < n_z:
@@ -196,28 +213,54 @@
         if 0 <= step - 2 < n_z:
             stage_c(step - 2)
 
-    for k in range(1, n_z):
-        es = lax.rem(e + k, n_z)
-        partial(es, es).wait_recv()
-    gate = jnp.zeros((total, half), jnp.float32)
-    up = jnp.zeros((total, half), jnp.float32)
-    for k in range(n_z):
-        gate = gate + part_in[k, 0].astype(jnp.float32)
-        up = up + part_in[k, 1].astype(jnp.float32)
-    act = gate / (1.0 + jnp.exp(-gate)) * up * jnp.abs(signs(e))
-    hid[e] = act.astype(jnp.bfloat16)
-    for k in range(1, n_z):
-        hidden(lax.rem(e + k, n_z), e).start()
+    def combine(b, down):
+        begin, end = (last_z, 0) if down else (0, last_z)
+        to, back = (prev_z, next_z) if down else (next_z, prev_z)
+
+        @pl.when((e != begin) & (e != end))
+        def _():
+            for c in range(2 * tiles):
+                partial(b, c, back).wait_recv()
+                value = part[b, c] + run_in[b, c].astype(jnp.float32)
+                run_out[b, c] = value.astype(jnp.bfloat16)
+                partial(b, c, to).start()
+
+        @pl.when(e == end)
+        def _():
+            for c in range(2 * tiles):
+                partial(b, c, back).wait_recv()
+            scale = jnp.abs(signs(b))
+            for c in range(tiles):
+                gate = part[b, c] + run_in[b, c].astype(jnp.float32)
+                up = part[b, tiles + c] + run_in[b, tiles + c].astype(jnp.float32)
+                act = gate / (1.0 + jnp.exp(-gate)) * up * scale
+                hid[b, c] = act.astype(jnp.bfloat16)
+                hidden(b, c, back).start()
+
+    def relay(b, down):
+        begin, end = (last_z, 0) if down else (0, last_z)
+        to, back = (prev_z, next_z) if down else (next_z, prev_z)
+        for c in range(tiles):
+
+            @pl.when(e != end)
+            def _():
+                hidden(b, c, to).wait_recv()
+
+            @pl.when((e != end) & (e != begin))
+            def _():
+                hidden(b, c, back).start()
+
+    for b, down in order:
+        combine(b, down)
 
     load_out.wait()
     wide = 256 if width % 256 == 0 else width
 
     def stage_d(k):
-        es = lax.rem(e + k, n_z)
-        if k > 0:
-            hidden(es, es).wait_recv()
+        es = order[k][0]
+        relay(*order[k])
         second = signs(es) < 0
-        h = hid[es].astype(jnp.float32)
+        h = jnp.concatenate([hid[es, c] for c in range(tiles)], axis=-1).astype(jnp.float32)
         h0 = jnp.where(second, 0.0, h).astype(jnp.bfloat16)
         h1 = jnp.where(second, h, 0.0).astype(jnp.bfloat16)
 
@@ -238,7 +281,7 @@
         sibling(es).start()
 
     def stage_e(k):
-        es = lax.rem(e + k, n_z)
+        es = order[k][0]
         sibling(es).wait_recv()
         both = o_both[es, p].astype(jnp.float32) + o_sib[es].astype(jnp.float32)
         x_out[es] = both.astype(jnp.bfloat16)
@@ -246,16 +289,21 @@
             reduce_x(es, lax.rem(t + i, n_t), t).start()
 
     def stage_f(k):
-        es = lax.rem(e + k, n_z)
+        es = order[k][0]
         value = x_out[es, t].astype(jnp.float32)
         for i in range(1, n_t):
             ts = lax.rem(t + i, n_t)
             reduce_x(es, ts, ts).wait_recv()
             value = value + x_in[es, ts].astype(jnp.float32)
-        if k == 0:
-            z_in[e] = value.astype(jnp.bfloat16)
-        else:
-            z_out[es] = value.astype(jnp.bfloat16)
+        value = value.astype(jnp.bfloat16)
+
+        @pl.when(e == es)
+        def _():
+            z_in[es] = value
+
+        @pl.when(e != es)
+        def _():
+            z_out[es] = value
             deliver(es, e).start()
 
     for step in range(n_z + 2):
@@ -298,12 +346,23 @@
     for k in range(1, n_z):
         es = lax.rem(e + k, n_z)
         across(es, es, e).wait_send()
-        partial(es, e).wait_send()
-        hidden(es, e).wait_send()
         deliver(es, e).wait_send()
     for b in range(n_z):
         pair(b, p).wait_send()
         sibling(b).wait_send()
+    for b, down in order:
+        begin, end = (last_z, 0) if down else (0, last_z)
+        to, back = (prev_z, next_z) if down else (next_z, prev_z)
+
+        @pl.when(e != end)
+        def _():
+            for c in range(2 * tiles):
+                partial(b, c, to).wait_send()
+
+        @pl.when(e != begin)
+        def _():
+            for c in range(tiles):
+                hidden(b, c, back).wait_send()
 
 
 def local(
@@ -331,6 +390,8 @@
 
     total = 2 * n_t * rows
     long = width + LANES
+    tile = min(half, 256)
+    tiles = half // tile
     b16 = jnp.bfloat16
     dma = pltpu.SemaphoreType.DMA
     sems = [
@@ -339,8 +400,8 @@
         dma((n_z,)), dma((n_z,)),
         dma((n_z, n_t)), dma((n_z, n_t)),
         dma((n_z,)), dma((n_z,)),
-        dma((n_z,)), dma((n_z,)),
-        dma((n_z,)), dma((n_z,)),
+        dma((n_z, 2 * tiles)), dma((n_z, 2 * tiles)),
+        dma((n_z, tiles)), dma((n_z, tiles)),
         dma((n_z,)), dma((n_z,)),
         dma((n_z, n_t)), dma((n_z, n_t)),
         dma((n_z,)), dma((n_z,)),
@@ -361,9 +422,10 @@
             vmem(out_weights.shape, b16),
             vmem((n_t, n_r, rows, long), b16),
             vmem((n_z, 2, n_t, rows, long), b16),
-            vmem((n_z, 2, total, half), b16),
-            vmem((n_z, 2, total, half), b16),
-            vmem((n_z, total, half), b16),
+            vmem((n_z, 2 * tiles, total, tile), jnp.float32),
+            vmem((n_z, 2 * tiles, total, tile), b16),
+            vmem((n_z, 2 * tiles, total, tile), b16),
+            vmem((n_z, tiles, total, tile), b16),
             vmem((n_z, 2, n_t, rows, width), b16),
             vmem((n_z, n_t, rows, width), b16),
             vmem((n_z, n_t, rows, width), b16),

time: 143 us -> 143 us (level)
  no operation moved by 1% of the time
where the time goes in v3:
time: 143 us; the launch traced here: 142 us
  Pallas kernels  124 us (87%)
  local copies, waits for them, and re-layouts  12.4 us (9%)
  other arithmetic  4.74 us (3%)
    pallas_call x1, Pallas kernels, local(): pl.pallas_call(functools.partial(kernel, n_t, n_z, n_r, rows, width, half...  124 us
    unnamed x2, local copies, waits for them, and re-layouts  8.2 us

profile of v3, /device:TPU:10, one launch (start us, length us, event | category | flops | bytes accessed | tf_op | source)
XLA Modules:
  0.0 141.6 jit_solution(15074986597353859491)
XLA Ops:
  0.0 0.7 convert_element_type.17
  0.7 0.7 iota_compare_fusion.2
  1.4 0.7 iota_compare_fusion.1
  2.1 0.1 pad_add_fusion
  2.2 0.7 iota_add_fusion
  2.9 0.8 add_clamp_fusion
  3.7 0.1 convert_reduce_fusion
  3.8 0.1 convert_element_type.19
  3.9 0.1 broadcast_in_dim.2
  4.0 2.1 %reshape.50 = bf16[2,48,2,1792]{3,2,1,0:T(2,128)(2,1)S(1)} reshape(bf16[96,3584]{1,0:T(8,128)(2,1)} %param.8) | data formatting | bytes 1376256 | tf_op jit(solution)/shard_map/reshape | solution.py:387
  6.2 0.1 copy.20
  6.2 0.9 pad_maximum_fusion.xs
  7.2 7.3 %copy.19 = bf16[2,1792,2,512]{3,1,2,0:T(8,128)(2,1)} copy(bf16[2,1792,2,512]{3,2,1,0:T(2,128)(2,1)} %param.14) | data formatting | bytes 14680064 | tf_op args[6]
  14.4 124.4 %shard_map.82 = bf16[2,2,48,1792]{3,2,1,0:T(8,128)(2,1)} custom-call(bf16[2,2,48,1920]{3,2,1,0:T(8,128)(2,1)} %pad_maximum_fusion.xs, bf16[2,2,1792,512]{3,2,1,0:T(8,128)(2,1)} %bitcast.14, bf16[2,512,1792]{2,1,0:T(8,128)(2,1)} %w_out.1), custom_call_target="tpu_custom_call" | custom-call | tf_op jit(solution)/shard_map/pallas_call | solution.py:411
  138.9 1.8 %copy.15 = bf16[2,48,2,1792]{3,2,1,0:T(2,128)(2,1)S(1)} copy(bf16[2,48,2,1792]{3,1,0,2:T(8,128)(2,1)} %bitcast.17) | data formatting | bytes 1376256 | tf_op jit(solution)/shard_map/transpose | solution.py:441
  140.7 0.9 copy.16
  (2 shorter events, 0.0 us)

commit v4 on v3

--- a/solution.py
+++ b/solution.py
@@ -11,27 +11,33 @@
 LANES = 128
 
 
-def token_scales(route_weight, starts, counts, spills, spill_counts):
-    rows_each = route_weight.shape[0]
+def signed_scales(count_rows, padded, weight, starts, counts, spills, spill_counts):
     overflow = spills.shape[-1]
-    capacity = rows_each - overflow
-    first_pos = jnp.arange(capacity, dtype=jnp.int32)
-    spill_pos = jnp.arange(overflow, dtype=jnp.int32)
-    slot_rows = jnp.clip(
-        jnp.concatenate([starts[:, None] + first_pos, spills], axis=-1), 0, rows_each - 1
-    )
-    slot_live = jnp.concatenate(
-        [first_pos < counts[:, None], spill_pos < spill_counts[:, None]], axis=-1
-    )
-    hits = (slot_rows[:, :, None] == jnp.arange(rows_each)) & slot_live[:, :, None]
-    live = jnp.sum(hits.astype(jnp.float32), axis=1)
-    return live * route_weight.astype(jnp.float32)
+    capacity = count_rows - overflow
+    sums = []
+    for ex in range(2):
+        row = lax.broadcasted_iota(jnp.int32, (padded, capacity), 0)
+        pos = lax.broadcasted_iota(jnp.int32, (padded, capacity), 1)
+        slot = jnp.clip(starts[:, ex : ex + 1] + pos, 0, count_rows - 1)
+        hit = jnp.where((slot == row) & (pos < counts[:, ex : ex + 1]), 1.0, 0.0)
+        row = lax.broadcasted_iota(jnp.int32, (padded, overflow), 0)
+        pos = lax.broadcasted_iota(jnp.int32, (padded, overflow), 1)
+        slot = jnp.clip(spills[ex : ex + 1, :], 0, count_rows - 1)
+        more = jnp.where((slot == row) & (pos < spill_counts[:, ex : ex + 1]), 1.0, 0.0)
+        sums.append(
+            jnp.sum(hit, axis=1, keepdims=True) + jnp.sum(more, axis=1, keepdims=True)
+        )
+    row = lax.broadcasted_iota(jnp.int32, (padded, padded), 0)
+    col = lax.broadcasted_iota(jnp.int32, (padded, padded), 1)
+    weight = jnp.broadcast_to(weight.astype(jnp.float32), (padded, padded))
+    column = jnp.sum(jnp.where(row == col, weight, 0.0), axis=1, keepdims=True)
+    return (sums[0] - sums[1]) * column
 
 
 def kernel(
-    n_t, n_z, n_r, rows, width, half,
-    xs, w_in, w_out, out_ref,
-    wi, wo, first, x_all, part, run_out, run_in, hid, o_both, o_sib, x_out, x_in, z_out, z_in, last,
+    n_t, n_z, n_r, rows, width, half, rows_each,
+    tokens, weight, starts, counts, spills, spill_counts, w_in, w_out, out_ref,
+    xs, wi, wo, first, x_all, part, run_out, run_in, hid, o_both, o_sib, x_out, x_in, z_out, z_in, last,
     wsem, lsem, s0, r0, s1, r1, s2, r2, s3, r3, s4, r4, s5, r5, s6, r6, s7, r7, s8, r8, s9, r9,
 ):
     e = lax.axis_index("expert")
@@ -43,7 +49,6 @@
     load_in = pltpu.make_async_copy(w_in, wi, wsem.at[0])
     load_out = pltpu.make_async_copy(w_out, wo, wsem.at[1])
     own_piece = pltpu.make_async_copy(xs.at[t], first.at[t], lsem.at[0])
-    own_piece.start()
     load_in.start()
     load_out.start()
 
@@ -57,6 +62,16 @@
             barrier, inc=1, device_id={"expert": lax.rem(e + k, n_z)}, device_id_type=MESH
         )
     pl.semaphore_signal(barrier, inc=1, device_id={"dp": other}, device_id_type=MESH)
+    signed = signed_scales(
+        rows_each, n_t * rows, weight[...], starts[...], counts[...], spills[...], spill_counts[...]
+    )
+    meta = jnp.broadcast_to(signed, (n_t * rows, LANES)).astype(jnp.bfloat16)
+    for i in range(n_t):
+        piece = slice(i * rows, (i + 1) * rows)
+        for j in range(n_r):
+            xs[i, j, :, :LANES] = meta[piece]
+            xs[i, j, :, LANES:] = tokens[piece, j * width : (j + 1) * width]
+    own_piece.start()
     pl.semaphore_wait(barrier, n_t + n_z - 1)
 
     def remote(src, dst, send, recv, **where):
@@ -258,7 +273,6 @@
 
     def stage_d(k):
         es = order[k][0]
-        relay(*order[k])
         second = signs(es) < 0
         h = jnp.concatenate([hid[es, c] for c in range(tiles)], axis=-1).astype(jnp.float32)
         h0 = jnp.where(second, 0.0, h).astype(jnp.bfloat16)
@@ -307,9 +321,14 @@
             deliver(es, e).start()
 
     for step in range(n_z + 2):
+        if step > 0 and step % 2 == 0 and step - 1 < n_z:
+            stage_e(step - 1)
         if step < n_z:
+            if step == 0:
+                for b, down in order:
+                    relay(b, down)
             stage_d(step)
-        if 0 <= step - 1 < n_z:
+        if 0 <= step - 1 < n_z and step % 2 == 1:
             stage_e(step - 1)
         if 0 <= step - 2 < n_z:
             stage_f(step - 2)
@@ -333,7 +352,9 @@
         ts = lax.rem(t + k, n_t)
         for j in range(n_r):
             finish(0, ts, j, ts).wait_recv()
-    out_ref[...] = last[...]
+    for i in range(n_t):
+        for j in range(n_r):
+            out_ref[i * rows : (i + 1) * rows, j * width : (j + 1) * width] = last[j, i]
 
     for k in range(1, n_t):
         ts = lax.rem(t + k, n_t)
@@ -374,18 +395,11 @@
     n_r = n_z // n_t
     width = in_weights.shape[1]
     half = in_weights.shape[3]
-    scales = token_scales(
-        route_weight, block_start[0], block_count[0], spill_rows[0], spill_count[0]
-    )
-    signed = (scales[0] - scales[1]).astype(jnp.bfloat16)
     rows = -(-rows_each // (16 * n_t)) * 16
     extra = rows * n_t - rows_each
     if extra:
         tokens = jnp.pad(tokens, ((0, extra), (0, 0)))
-        signed = jnp.pad(signed, (0, extra))
-    meta = jnp.broadcast_to(signed.reshape(n_t, 1, rows, 1), (n_t, n_r, rows, LANES))
-    blocks = tokens.reshape(n_t, rows, n_r, width).transpose(0, 2, 1, 3)
-    xs = jnp.concatenate([meta, blocks], axis=-1)
+        route_weight = jnp.pad(route_weight, (0, extra))
     w_in = in_weights.transpose(0, 2, 1, 3)
 
     total = 2 * n_t * rows
@@ -409,15 +423,21 @@
     ]
     vmem = pltpu.VMEM
     out = pl.pallas_call(
-        functools.partial(kernel, n_t, n_z, n_r, rows, width, half),
-        out_shape=jax.ShapeDtypeStruct((n_r, n_t, rows, width), b16),
+        functools.partial(kernel, n_t, n_z, n_r, rows, width, half, rows_each),
+        out_shape=jax.ShapeDtypeStruct((n_t * rows, cols), b16),
         in_specs=[
+            pl.BlockSpec(memory_space=pltpu.VMEM),
+            pl.BlockSpec(memory_space=pltpu.VMEM),
+            pl.BlockSpec(memory_space=pltpu.VMEM),
+            pl.BlockSpec(memory_space=pltpu.VMEM),
+            pl.BlockSpec(memory_space=pltpu.VMEM),
             pl.BlockSpec(memory_space=pltpu.VMEM),
             pl.BlockSpec(memory_space=pl.ANY),
             pl.BlockSpec(memory_space=pl.ANY),
         ],
         out_specs=pl.BlockSpec(memory_space=pltpu.VMEM),
         scratch_shapes=[
+            vmem((n_t, n_r, rows, long), b16),
             vmem(w_in.shape, b16),
             vmem(out_weights.shape, b16),
             vmem((n_t, n_r, rows, long), b16),
@@ -437,8 +457,16 @@
         compiler_params=pltpu.CompilerParams(
             collective_id=0, has_side_effects=True, vmem_limit_bytes=56 * 1024 * 1024
         ),
-    )(xs, w_in, out_weights)
-    out = out.transpose(1, 2, 0, 3).reshape(n_t * rows, cols)
+    )(
+        tokens,
+        route_weight[None],
+        block_start,
+        block_count,
+        spill_rows[0],
+        spill_count,
+        w_in,
+        out_weights,
+    )
     return out[:rows_each]
 
 

time: 143 us -> 134 us (0.937)
  other arithmetic: 4.74 us -> 0 us
  local copies, waits for them, and re-layouts: 12.4 us -> 9.27 us
    reshape x2 -> x0, local copies, waits for them, and re-layouts: 2.2 us -> none  [local(): blocks = tokens.reshape(n_t, rows, n_r, width).transpose(0, 2, 1, 3)]
    transpose x1 -> x0, local copies, waits for them, and re-layouts: 1.81 us -> none  [local(): out = out.transpose(1, 2, 0, 3).reshape(n_t * rows, cols)]
    pallas_call x1, Pallas kernels: 124 us -> 123 us  [local(): pl.pallas_call(functools.partial(kernel, n_t, n_z, n_r, rows, width, half...]
    lt x2 -> x0, other arithmetic: 1.45 us -> none  [the longest x1 0.73 us: token_scales(): first_pos < counts[:, None]]
where the time goes in v4:
time: 134 us; the launch traced here: 132 us
  Pallas kernels  123 us (92%)
  local copies, waits for them, and re-layouts  9.27 us (7%)
    pallas_call x1, Pallas kernels, local(): pl.pallas_call(functools.partial(kernel, n_t, n_z, n_r, rows, width, half...  123 us
    unnamed x2, local copies, waits for them, and re-layouts  9.27 us

profile of v4, /device:TPU:10, one launch (start us, length us, event | category | flops | bytes accessed | tf_op | source)
XLA Modules:
  0.0 132.0 jit_solution(4416028162002680)
XLA Ops:
  0.0 7.3 %copy.11 = bf16[2,1792,2,512]{3,1,2,0:T(8,128)(2,1)} copy(bf16[2,1792,2,512]{3,2,1,0:T(2,128)(2,1)} %param.14) | data formatting | bytes 14680064 | tf_op args[6]
  7.3 122.7 %shard_map.82 = bf16[96,3584]{1,0:T(8,128)(2,1)} custom-call(bf16[96,3584]{1,0:T(8,128)(2,1)} %tokens.1, bf16[1,96]{1,0:T(2,128)(2,1)} %bitcast.7, s32[1,2]{1,0:T(1,128)} %starts.1, s32[1,2]{1,0:T(1,128)} %counts.1, s32[2,32]{1,0:T(2,128)} %bitcast.6, s32[1,2]{1,0:T(1,128)} %spill_counts.1, bf16[2,2,1792,512]{3,2,1,0:T(8,128)(2,1)} %bitcast.5, ...), custom_call_target="tpu_custom_call" | custom-call | tf_op jit(solution)/shard_map/pallas_call | solution.py:425
  130.0 2.0 %copy.13 = bf16[96,3584]{1,0:T(8,128)(2,1)} copy(bf16[96,3584]{1,0:T(8,128)(2,1)} %shard_map.82) | data formatting | bytes 1376256

commit v5 on v4

--- a/solution.py
+++ b/solution.py
@@ -455,7 +455,7 @@
             vmem((n_r, n_t, rows, width), b16),
         ] + sems,
         compiler_params=pltpu.CompilerParams(
-            collective_id=0, has_side_effects=True, vmem_limit_bytes=56 * 1024 * 1024
+            collective_id=0, has_side_effects=True, vmem_limit_bytes=40 * 1024 * 1024
         ),
     )(
         tokens,

time: 134 us -> 129 us (0.963)
  local copies, waits for them, and re-layouts: 9.27 us -> 5.41 us
    unnamed x2 -> x16, local copies, waits for them, and re-layouts: 9.27 us -> 5.41 us
where the time goes in v5:
time: 129 us; the launch traced here: 127 us
  Pallas kernels  122 us (95%)
  local copies, waits for them, and re-layouts  5.41 us (4%)
    pallas_call x1, Pallas kernels, local(): pl.pallas_call(functools.partial(kernel, n_t, n_z, n_r, rows, width, half...  122 us
    unnamed x16, local copies, waits for them, and re-layouts  5.41 us

profile of v5, /device:TPU:10, one launch (start us, length us, event | category | flops | bytes accessed | tf_op | source)
XLA Modules:
  0.0 127.1 jit_solution(6193027627565439287)
XLA Ops:
  0.0 0.0 copy-start
  0.0 0.0 copy-start.1
  0.0 0.0 copy-start.2
  0.0 0.0 copy-start.3
  0.0 0.0 copy-start.4
  0.0 0.0 copy-start.5
  0.0 0.0 copy-start.6
  0.0 4.5 %copy.11 = bf16[2,1792,2,512]{3,1,2,0:T(8,128)(2,1)S(1)} copy(bf16[2,1792,2,512]{3,2,1,0:T(2,128)(2,1)} %param.14) | data formatting | bytes 14680064 | tf_op args[6]
  4.6 0.0 copy-done
  4.6 0.0 copy-done.1
  4.6 0.0 copy-done.2
  4.6 0.0 copy-done.3
  4.6 0.0 copy-done.4
  4.6 0.0 copy-done.5
  4.6 0.0 copy-done.6
  4.7 121.6 %shard_map.82 = bf16[96,3584]{1,0:T(8,128)(2,1)S(1)} custom-call(bf16[96,3584]{1,0:T(8,128)(2,1)S(1)} %copy-done.1, bf16[1,96]{1,0:T(2,128)(2,1)S(1)} %bitcast.7, s32[1,2]{1,0:T(1,128)S(1)} %copy-done.4, s32[1,2]{1,0:T(1,128)S(1)} %copy-done.5, s32[2,32]{1,0:T(2,128)S(1)} %bitcast.6, s32[1,2]{1,0:T(1,128)S(1)} %copy-done.6, ...), custom_call_target="tpu_custom_call" | custom-call | tf_op jit(solution)/shard_map/pallas_call | solution.py:425
  126.2 0.8 copy.13
Async XLA Ops:
  0.0 4.6 %copy-start = (bf16[2,512,1792]{2,1,0:T(8,128)(2,1)S(1)}, bf16[2,512,1792]{2,1,0:T(8,128)(2,1)}, u32[]{:S(2)}) copy-start(bf16[2,512,1792]{2,1,0:T(8,128)(2,1)} %w_out.1) | copy-start | bytes 11010052
  0.0 4.6 %copy-start.1 = (bf16[96,3584]{1,0:T(8,128)(2,1)S(1)}, bf16[96,3584]{1,0:T(8,128)(2,1)}, u32[]{:S(2)}) copy-start(bf16[96,3584]{1,0:T(8,128)(2,1)} %tokens.1) | copy-start | bytes 2064388
  0.0 4.6 %copy-start.2 = (s32[1,2,32]{2,1,0:T(2,128)S(1)}, s32[1,2,32]{2,1,0:T(2,128)}, u32[]{:S(2)}) copy-start(s32[1,2,32]{2,1,0:T(2,128)} %param.12) | copy-start | bytes 772
  0.0 4.6 %copy-start.3 = (bf16[96]{0:T(256)(128)(2,1)S(1)}, bf16[96]{0:T(256)(128)(2,1)}, u32[]{:S(2)}) copy-start(bf16[96]{0:T(256)(128)(2,1)} %param.9) | copy-start | bytes 580
  0.0 4.6 %copy-start.4 = (s32[1,2]{1,0:T(1,128)S(1)}, s32[1,2]{1,0:T(1,128)}, u32[]{:S(2)}) copy-start(s32[1,2]{1,0:T(1,128)} %starts.1) | copy-start | bytes 28
  0.0 4.6 %copy-start.5 = (s32[1,2]{1,0:T(1,128)S(1)}, s32[1,2]{1,0:T(1,128)}, u32[]{:S(2)}) copy-start(s32[1,2]{1,0:T(1,128)} %counts.1) | copy-start | bytes 28
  0.0 4.6 %copy-start.6 = (s32[1,2]{1,0:T(1,128)S(1)}, s32[1,2]{1,0:T(1,128)}, u32[]{:S(2)}) copy-start(s32[1,2]{1,0:T(1,128)} %spill_counts.1) | copy-start | bytes 28
